TPU v7x, 32 devices: a whole 2x2x4 slice. The times are simulated.
32 devices in a mesh: groups: 2 (over x), mp: 8 (over z, y), dp: 2 (over core).
Axes of the slice: x: 2, y: 2, z: 4, core: 2. Of those that a mesh axis runs over, the one named last changes fastest.
Arguments:
- activations: bfloat16 [2048, 8192], P(('groups', 'dp'), 'mp'), parts along dimension 0, may hold values from -6 to 6
- cotangent: bfloat16 [2048, 14336], P(('groups', 'dp'), 'mp'), parts along dimension 0, may hold values from -6 to 6
- frozen_weight: bfloat16 [8192, 14336], P(None, 'mp'), may hold values from -0.09375 to 0.09375
- adapter_down: bfloat16 [8192, 64], P('mp'), may hold values from -0.0625 to 0.0625
- adapter_up: bfloat16 [64, 14336], P(None, 'mp'), may hold values from -0.75 to 0.75
- sparse_values: bfloat16 [64, 8, 128, 128], P('mp'), may hold values from -0.5 to 0.5
- block_cols: int32 [64, 8], replicated, may hold values from 0 to 111, as said below
- block_count: int32 [64], replicated, may hold values from 0 to 2, as said below
Outputs:
- input_grad: bfloat16 [2048, 8192], P(('groups', 'dp'), 'mp'), parts along dimension 0
- down_grad: float32 [16384, 64], P(('groups', 'mp')), parts along dimension 0
- up_grad: float32 [128, 14336], P('groups', 'mp'), parts along dimension 0
- block_grads: float32 [128, 8, 128, 128], P(('groups', 'mp'), 'dp'), parts along dimension 0
There are 2 independent parts, one for each index of `groups`. A program takes and returns all parts, laid end to end along the dimension named above; an argument that names none is the same for every part. Nothing has to cross between parts.
Inputs may be any that keep to these rules, and one draw needn't show every extreme that they name: `block_cols`: the first block_count[r] entries of block row r are distinct and increasing; the others are 0. Cut the block rows into aligned runs of 8 and the block columns into aligned runs of 14: no run of rows has more than 2 support blocks in one run of columns, and in every run of rows some run of columns has exactly 2. `block_count`: some block row has exactly 2 support blocks.
All inputs are finite; a program needn't handle non-finite values.
Results may differ from a plain program's by a relative error of at most 0.015.
Values may be sent and summed in bfloat16 or wider, within the bound.
A program may use at most 128 MiB of HBM per device.

v0:
```python
import jax
import jax.numpy as jnp
from jax import lax
from jax.sharding import PartitionSpec as P

BLK = 128
MAXR = 8
CAP = 2


adapter_scale = 0.125


def slot_tables(block_cols, block_count, mp_count, per_owner, per_holder):
    col_table = block_cols.reshape(mp_count, per_owner * MAXR)
    slot_ids = jnp.tile(jnp.arange(MAXR, dtype=jnp.int32), per_owner)
    counts_wide = jnp.repeat(block_count.reshape(mp_count, per_owner), MAXR, axis=1)
    valid_slots = slot_ids[None, :] < counts_wide
    holder = col_table // per_holder
    block_ids = jnp.arange(per_owner * MAXR, dtype=jnp.int32)
    earlier = block_ids[None, :] < block_ids[:, None]
    same_holder = (
        (holder[:, :, None] == holder[:, None, :]) & valid_slots[:, None, :] & earlier[None, :, :]
    )
    slot_rank = jnp.sum(same_holder.astype(jnp.int32), axis=2)
    return (col_table, valid_slots, holder, slot_rank)


def outgoing(col_table, valid_slots, holder, slot_rank, my_index, per_holder):
    capacity_ids = jnp.arange(CAP, dtype=jnp.int32)
    picked = (
        valid_slots[:, :, None]
        & (holder == my_index)[:, :, None]
        & (slot_rank[:, :, None] == capacity_ids[None, None, :])
    )
    local_cols = (col_table - my_index * per_holder)[:, :, None]
    return jnp.sum(jnp.where(picked, local_cols, 0), axis=1).reshape(-1)


def local(
    activations,
    cotangent,
    frozen_weight,
    adapter_down,
    adapter_up,
    sparse_values,
    block_cols,
    block_count,
):
    tok_rows, width_own = activations.shape
    mp_count = lax.axis_size("mp")
    my_index = lax.axis_index("mp")
    per_owner = width_own // BLK
    per_holder = cotangent.shape[1] // BLK
    loss_scale = (tok_rows * lax.axis_size("dp")) ** (-0.5)
    contract_last = (((1,), (1,)), ((), ()))
    contract_first = (((0,), (0,)), ((), ()))
    down_part = jnp.dot(activations, adapter_down, preferred_element_type=jnp.float32)
    up_part = lax.dot_general(
        cotangent, adapter_up, contract_last, preferred_element_type=jnp.float32
    )
    down_total, up_total = (
        lax.psum(down_part.astype(jnp.bfloat16), "mp").astype(jnp.float32),
        lax.psum(up_part.astype(jnp.bfloat16), "mp").astype(jnp.float32),
    )
    low16 = down_total.astype(jnp.bfloat16)
    back16 = (adapter_scale * up_total).astype(jnp.bfloat16)
    col_table, valid_slots, holder, slot_rank = slot_tables(
        block_cols, block_count, mp_count, per_owner, per_holder
    )
    my_valid = lax.dynamic_index_in_dim(valid_slots, my_index, 0, keepdims=False)
    my_holder = lax.dynamic_index_in_dim(holder, my_index, 0, keepdims=False)
    my_rank = lax.dynamic_index_in_dim(slot_rank, my_index, 0, keepdims=False)
    recv_index = jnp.where(my_valid, my_holder * CAP + jnp.minimum(my_rank, CAP - 1), 0)
    used_mask = my_valid.reshape(per_owner, MAXR).astype(jnp.float32)
    act_blocks = jnp.transpose(activations.reshape(tok_rows, per_owner, BLK), (1, 0, 2))
    cot_blocks = jnp.transpose(cotangent.reshape(tok_rows, per_holder, BLK), (1, 0, 2))
    wanted = outgoing(col_table, valid_slots, holder, slot_rank, my_index, per_holder)
    sent_cols = jnp.take(cot_blocks, wanted, axis=0).reshape(mp_count, CAP, tok_rows, BLK)
    got_cols = lax.all_to_all(sent_cols, "mp", split_axis=0, concat_axis=0, tiled=True)
    row_cols = jnp.take(got_cols.reshape(-1, tok_rows, BLK), recv_index, axis=0).reshape(
        per_owner, MAXR, tok_rows, BLK
    )
    block_part = loss_scale * jnp.einsum(
        "atb,aktc->akbc", act_blocks, row_cols, preferred_element_type=jnp.float32
    )
    block_part = block_part * used_mask[:, :, None, None]
    masked_values = jnp.where(
        used_mask[:, :, None, None] > 0.0, sparse_values, jnp.zeros_like(sparse_values)
    )
    sparse_part = jnp.einsum(
        "aktc,akbc->atb", row_cols, masked_values, preferred_element_type=jnp.float32
    )
    dense_cols = lax.psum_scatter(
        lax.dot_general(
            frozen_weight, cotangent, contract_last, preferred_element_type=jnp.float32
        ).astype(jnp.bfloat16),
        "mp",
        scatter_dimension=0,
        tiled=True,
    ).astype(jnp.float32)
    adapter_term = lax.dot_general(
        back16, adapter_down, contract_last, preferred_element_type=jnp.float32
    )
    sparse_flat = jnp.transpose(sparse_part, (1, 0, 2)).reshape(tok_rows, width_own)
    input_grad = (jnp.transpose(dense_cols) + sparse_flat + adapter_term).astype(jnp.bfloat16)
    down_local = loss_scale * lax.dot_general(
        activations, back16, contract_first, preferred_element_type=jnp.float32
    )
    up_local = (
        loss_scale
        * adapter_scale
        * lax.dot_general(low16, cotangent, contract_first, preferred_element_type=jnp.float32)
    )
    down_grad, up_grad = (
        lax.psum(down_local.astype(jnp.bfloat16), "dp").astype(jnp.float32),
        lax.psum(up_local.astype(jnp.bfloat16), "dp").astype(jnp.float32),
    )
    half_slots = MAXR // lax.axis_size("dp")
    whole_sum = lax.psum(block_part.astype(jnp.bfloat16), "dp").astype(jnp.float32)
    block_grads = lax.dynamic_slice_in_dim(
        whole_sum, lax.axis_index("dp") * half_slots, half_slots, 1
    )
    return (input_grad, down_grad, up_grad, block_grads)


def solution(mesh):
    return jax.shard_map(
        local,
        mesh=mesh,
        in_specs=(
            P(("groups", "dp"), "mp"),
            P(("groups", "dp"), "mp"),
            P(None, "mp"),
            P("mp", None),
            P(None, "mp"),
            P("mp", None, None, None),
            P(),
            P(),
        ),
        out_specs=(
            P(("groups", "dp"), "mp"),
            P(("groups", "mp"), None),
            P("groups", "mp"),
            P(("groups", "mp"), "dp", None, None),
        ),
        check_vma=False,
    )
```

profile of v0, /device:TPU:1, one launch (start us, length us, event | category | flops | bytes accessed | tf_op | source)
XLA Modules:
  0.0 336.8 jit_solution(7995003695594816304)
XLA Ops:
  11.0 3.8 %copy.32 = bf16[512,1792]{0,1:T(8,128)(2,1)} copy(bf16[512,1792]{1,0:T(8,128)(2,1)} %param.9) | data formatting | bytes 3670016 | tf_op args[1]
  14.8 2.9 copy.33
  17.7 2.1 gather_fusion
  19.9 3.2 broadcast_select_fusion.3
  23.0 6.5 %all-to-all-start = ((bf16[8,2,512,128]{3,2,1,0:T(8,128)(2,1)}), bf16[8,2,512,128]{3,2,1,0:T(8,128)(2,1)S(1)}, u32[]{:S(2)}, u32[]{:S(2)}) async-start(bf16[8,2,512,128]{3,2,1,0:T(8,128)(2,1)} %broadcast_select_fusion.3), calls=%async_computation.1 | async-start | bytes 4194304 | tf_op jit(solution)/shard_map/all_to_all | solution.py:80
  29.6 1.1 convolution_convert_fusion.1
  30.7 2.8 convolution_convert_fusion.2
  35.0 85.7 %all-reduce.5.cloned.1.call-done = (bf16[512,64]{0,1:T(8,128)(2,1)}, bf16[512,64]{0,1:T(8,128)(2,1)}) async-done(((bf16[512,64]{0,1:T(8,128)(2,1)}, bf16[512,64]{0,1:T(8,128)(2,1)}), (bf16[512,64]{0,1:T(8,128)(2,1)}, bf16[512,64]{0,1:T(8,128)(2,1)})) %all-reduce.5.cloned.1.call-update) | async-done | bytes 131088 | tf_op jit(solution)/shard_map/psum | solution.py:64
  120.7 1.8 fusion.11
  122.5 2.7 fusion.4
  125.2 5.3 %gather_fusion.1 = bf16[64,512,128]{2,1,0:T(8,128)(2,1)} fusion(bf16[16,512,128]{2,1,0:T(8,128)(2,1)S(1)} %bitcast.52, s32[1024]{0:T(1024)S(1)} %pad_clamp_fusion), kind=kCustom, calls=%fused_computation.1 | custom fusion | bytes 16777472 | tf_op jit(solution)/shard_map/jit(_take)/gather | solution.py:81
  130.4 11.4 %copy.35 = bf16[8,8,512,128]{2,3,1,0:T(8,128)(2,1)} copy(bf16[8,8,512,128]{3,2,1,0:T(8,128)(2,1)} %bitcast.53) | data formatting | bytes 16777216 | tf_op jit(solution)/shard_map/jit(_take)/gather | solution.py:81
  141.8 7.1 %fusion.5 = bf16[8,8,128,128]{2,3,1,0:T(8,128)(2,1)} fusion(f32[8,8]{1,0:T(8,128)S(1)} %mul.71, bf16[8,8,512,128]{2,3,1,0:T(8,128)(2,1)} %copy.35, pred[8,8]{1,0:T(8,128)(4,1)S(1)} %compare_and_fusion.1, bf16[512,1024]{1,0:T(8,128)(2,1)S(1)} %copy-done), kind=kOutput, calls=%fused_computation.11 | convolution fusion | flops 1080033280 | bytes 11534656 | tf_op jit(solution)/shard_map/atb,aktc->akbc/dot_general | solution.py:84
  149.2 1.2 copy-done.2
  150.4 21.2 %convolution_convert_fusion = bf16[8192,512]{1,0:T(8,128)(2,1)} fusion(bf16[8192,1792]{1,0:T(8,128)(2,1)} %param.10, bf16[512,1792]{1,0:T(8,128)(2,1)S(1)} %copy-done.2), kind=kOutput, calls=%fused_computation.2 | convolution fusion | flops 15036579840 | bytes 39583744 | tf_op jit(solution)/shard_map/dot_general | solution.py:95
  171.8 1.4 copy-done.6
  173.2 6.5 %fusion.1 = f32[8,512,128,1]{1,2,3,0:T(8,128)} fusion(bf16[8,8,512,128]{2,3,1,0:T(8,128)(2,1)} %copy.35, pred[8,8]{1,0:T(8,128)(4,1)S(1)} %compare_and_fusion.1, bf16[8,8,128,128]{3,2,1,0:T(8,128)(2,1)S(1)} %copy-done.6, pred[8,8]{1,0:T(8,128)(4,1)S(1)} %gt.16), kind=kOutput, calls=%fused_computation.5 | convolution fusion | flops 1078984704 | bytes 12583040 | tf_op jit(solution)/shard_map/aktc,akbc->atb/dot_general | solution.py:91
  179.7 1.6 convert_element_type.68
  181.3 1.7 convert_element_type.71
  183.0 1.5 dynamic-slice_convert_fusion
  184.5 1.8 copy.40
  186.3 140.3 %reduce-scatter.2.cloned.1.call-done = bf16[1024,512]{1,0:T(8,128)(2,1)} async-done(((bf16[8192,512]{1,0:T(8,128)(2,1)}), bf16[1024,512]{1,0:T(8,128)(2,1)}) %reduce-scatter.2.cloned.1.call-update) | async-done | bytes 1048592 | tf_op jit(solution)/shard_map/reduce_scatter | solution.py:94
  326.6 2.4 fusion.7
  329.0 1.3 copy.39
  (53 shorter events, 5.6 us)
Async XLA Ops:
  7.2 22.4 %copy-start = (bf16[512,1024]{1,0:T(8,128)(2,1)S(1)}, bf16[512,1024]{1,0:T(8,128)(2,1)}, u32[]{:S(2)}) copy-start(bf16[512,1024]{1,0:T(8,128)(2,1)} %param.8) | copy-start | bytes 3145732
  23.0 6.6 %copy-start.3 = (bf16[1024,64]{0,1:T(8,128)(2,1)S(1)}, bf16[1024,64]{0,1:T(8,128)(2,1)}, u32[]{:S(2)}) copy-start(bf16[1024,64]{0,1:T(8,128)(2,1)} %param.11) | copy-start | bytes 393220
  23.0 7.7 %copy-start.5 = (bf16[64,1792]{1,0:T(8,128)(2,1)S(1)}, bf16[64,1792]{1,0:T(8,128)(2,1)}, u32[]{:S(2)}) copy-start(bf16[64,1792]{1,0:T(8,128)(2,1)} %param.12) | copy-start | bytes 688132
  23.0 102.1 %all-to-all-start = ((bf16[8,2,512,128]{3,2,1,0:T(8,128)(2,1)}), bf16[8,2,512,128]{3,2,1,0:T(8,128)(2,1)S(1)}, u32[]{:S(2)}, u32[]{:S(2)}) async-start(bf16[8,2,512,128]{3,2,1,0:T(8,128)(2,1)} %broadcast_select_fusion.3), calls=%async_computation.1 | async-start | bytes 4194304 | tf_op jit(solution)/shard_map/all_to_all | solution.py:80
  29.5 91.2 %all-reduce.5.cloned.1.call-start = ((), (), s32[]{:S(2)}) async-start(), calls=%async_computation.3 | async-start | bytes 262144 | tf_op jit(solution)/shard_map/psum | solution.py:64
  33.5 146.1 %all-reduce.7.cloned.1.call-start = ((), (), s32[]{:S(2)}) async-start(), calls=%async_computation.4 | async-start | bytes 4915200 | tf_op jit(solution)/shard_map/psum | solution.py:116
  148.9 1.5 copy-start.2
  148.9 177.6 %reduce-scatter.2.cloned.1.call-start = ((), (), s32[]{:S(2)}) async-start(), calls=%async_computation.2 | async-start | bytes 9437184 | tf_op jit(solution)/shard_map/reduce_scatter | solution.py:94
  171.6 1.6 copy-start.6
  184.5 142.1 %copy-start.4 = (bf16[512,64]{0,1:T(8,128)(2,1)S(1)}, bf16[512,64]{0,1:T(8,128)(2,1)}, u32[]{:S(2)}) copy-start(bf16[512,64]{0,1:T(8,128)(2,1)} %get-tuple-element.16) | copy-start | bytes 196612
  326.6 3.7 %copy-start.1 = (bf16[512,1024]{1,0:T(8,128)(2,1)S(1)}, bf16[512,1024]{1,0:T(8,128)(2,1)}, u32[]{:S(2)}) copy-start(bf16[512,1024]{1,0:T(8,128)(2,1)} %param.8) | copy-start | bytes 3145732
Sparse Core Ops, SparseCore 0:
  34.4 86.2 all-reduce.4
  149.0 23.5 all-reduce.6
  176.7 149.8 reduce-scatter.1
where the time goes:
time: 338 us; the launch traced here: 337 us
  waiting for transfers between devices  226 us (67%)
  matrix products  45.5 us (13%)
  local copies, waits for them, and re-layouts  33.8 us (10%)
  between operations  13.9 us (4%)
  other arithmetic  10.7 us (3%)
  starting transfers between devices  6.82 us (2%)
    reduce_scatter x1, waiting for transfers between devices, local(): lax.psum_scatter(lax.dot_general(frozen_weight, cotangent, contract_last,...  140 us
    psum x1, waiting for transfers between devices, local(): lax.psum(up_part.astype(jnp.bfloat16), 'mp').astype(jnp.float32)  85.7 us
    dot_general x1, matrix products, local(): lax.dot_general(frozen_weight, cotangent, contract_last, preferred_elemen...  21.2 us
    gather x2, local copies, waits for them, and re-layouts, local(): jnp.take(got_cols.reshape(-1, tok_rows, BLK), recv_index, axis=0)  16.6 us
    unnamed x17, local copies, waits for them, and re-layouts  9.68 us
    dot_general x1, matrix products, local(): jnp.einsum('atb,aktc->akbc', act_blocks, row_cols, preferred_element_type...  7.09 us
  transfers between devices with their start and end apart: 4, of which 2 were waited for; matrix products, arithmetic and copies ran while one was open for 13% of the time, Pallas kernels for 0%

commit v1 on v0

v1 whole, which is shorter than its diff:
```python
import functools

import jax
import jax.numpy as jnp
import numpy as np
from jax import lax
from jax.experimental import pallas as pl
from jax.experimental.pallas import tpu as pltpu
from jax.sharding import PartitionSpec as P

BLK = 128
MAXR = 8
CAP = 2
PIECE = 256
INNER = 2
MESH = pl.DeviceIdType.MESH

adapter_scale = 0.125
contract_last = (((1,), (1,)), ((), ()))
contract_first = (((0,), (0,)), ((), ()))


def slot_tables(block_cols, block_count, mp_count, per_owner, per_holder):
    col_table = block_cols.reshape(mp_count, per_owner * MAXR)
    slot_ids = jnp.tile(jnp.arange(MAXR, dtype=jnp.int32), per_owner)
    counts_wide = jnp.repeat(block_count.reshape(mp_count, per_owner), MAXR, axis=1)
    valid_slots = slot_ids[None, :] < counts_wide
    holder = col_table // per_holder
    block_ids = jnp.arange(per_owner * MAXR, dtype=jnp.int32)
    earlier = block_ids[None, :] < block_ids[:, None]
    same_holder = (
        (holder[:, :, None] == holder[:, None, :]) & valid_slots[:, None, :] & earlier[None, :, :]
    )
    slot_rank = jnp.sum(same_holder.astype(jnp.int32), axis=2)
    return (col_table, valid_slots, holder, slot_rank)


def outgoing(col_table, valid_slots, holder, slot_rank, my_index, per_holder):
    capacity_ids = jnp.arange(CAP, dtype=jnp.int32)
    picked = (
        valid_slots[:, :, None]
        & (holder == my_index)[:, :, None]
        & (slot_rank[:, :, None] == capacity_ids[None, None, :])
    )
    local_cols = (col_table - my_index * per_holder)[:, :, None]
    return jnp.sum(jnp.where(picked, local_cols, 0), axis=1).reshape(-1)


def orders(outer):
    rows = []
    for z in range(outer):
        rows.append(sorted(range(outer), key=lambda d: (-abs(d - z), (d - z) if z % 2 else (z - d))))
    return np.array(rows, np.int32)


def kernel(
    n,
    wanted_ref, index_ref, valid_ref,
    act_ref, cot_ref, w_ref, down_ref, up_ref, values_ref,
    out_ref, down_out, up_out, blocks_out,
    wbuf, ysend, yrecv, own, zrecv, cotb, colsend, colgot, cat, vcat, sparse, bgtmp, bgkeep, bgsend, bgrecv,
    lbpart, lbgot, lbfull, dsend, drecv, usend, urecv,
    wsem, ys_sem, yr_sem, zs_sem, zr_sem, cs_sem, cr_sem, l1s, l1r, l2s, l2r, dps, dpr,
):
    me = lax.axis_index("mp")
    core = lax.axis_index("dp")
    tok, wide = act_ref.shape
    outer = n // INNER
    pieces = wide // PIECE
    rows = wide // BLK
    part = tok // n
    z, y = me // INNER, me % INNER
    pair = z * INNER + (1 - y)
    loss_scale = (tok * 2) ** (-0.5)
    table = orders(outer)

    def pick(step):
        total = jnp.int32(0)
        for i in range(outer):
            for s in range(outer):
                total = total + jnp.where((z == i) & (step == s), jnp.int32(int(table[i, s])), 0)
        return total

    def remote(src, dst, send, recv, mp=None, dp=None):
        target = {"mp": mp} if dp is None else {"dp": dp}
        return pltpu.make_async_remote_copy(
            src_ref=src, dst_ref=dst, send_sem=send, recv_sem=recv,
            device_id=target, device_id_type=MESH,
        )

    barrier = pltpu.get_barrier_semaphore()
    for j in range(1, n):
        pl.semaphore_signal(
            barrier, inc=1, device_id={"mp": lax.rem(me + j, n)}, device_id_type=MESH
        )
    pl.semaphore_signal(barrier, inc=1, device_id={"dp": 1 - core}, device_id_type=MESH)

    def item_owner(i):
        far = i < outer
        zd = pick(jnp.where(far, i, i - outer))
        return zd, zd * INNER + jnp.where(far, 1 - y, y)

    def fetch(i):
        _, owner = item_owner(i)
        slot = lax.rem(i, 2)
        return pltpu.make_async_copy(
            w_ref.at[pl.ds(pl.multiple_of(owner * wide, wide), wide), :], wbuf.at[slot], wsem.at[slot]
        )

    fetch(jnp.int32(0)).start()
    fetch(jnp.int32(1)).start()

    low_part = jnp.dot(act_ref[...], down_ref[...], preferred_element_type=jnp.float32)
    back_part = lax.dot_general(
        cot_ref[...], up_ref[...], contract_last, preferred_element_type=jnp.float32
    )
    lbpart[:, :, 0:64] = low_part.astype(jnp.bfloat16).reshape(n, part, 64)
    lbpart[:, :, 64:128] = back_part.astype(jnp.bfloat16).reshape(n, part, 64)
    pl.semaphore_wait(barrier, n)

    def lb1(j):
        dest = lax.rem(me + j, n)
        return remote(lbpart.at[dest], lbgot.at[me], l1s.at[dest], l1r.at[me], mp=dest)

    def lb1_in(j):
        src = lax.rem(me + j, n)
        return remote(lbpart.at[src], lbgot.at[src], l1s.at[src], l1r.at[src], mp=src)

    def lb2(j):
        dest = lax.rem(me + j, n)
        return remote(lbfull.at[me], lbfull.at[me], l2s.at[dest], l2r.at[me], mp=dest)

    def lb2_in(j):
        src = lax.rem(me + j, n)
        return remote(lbfull.at[src], lbfull.at[src], l2s.at[src], l2r.at[src], mp=src)

    def cols(j):
        dest = lax.rem(me + j, n)
        return remote(
            colsend.at[pl.ds(dest * CAP, CAP)], colgot.at[pl.ds(me * CAP, CAP)],
            cs_sem.at[dest], cr_sem.at[me], mp=dest,
        )

    def cols_in(j):
        src = lax.rem(me + j, n)
        return remote(
            colsend.at[pl.ds(src * CAP, CAP)], colgot.at[pl.ds(src * CAP, CAP)],
            cs_sem.at[src], cr_sem.at[src], mp=src,
        )

    def loop(count, body, start=0):
        def step(i, carry):
            body(i)
            return carry

        lax.fori_loop(start, count, step, 0)

    loop(n, lambda j: lb1(j).start(), 1)

    for i in range(cotb.shape[0]):
        cotb[i] = cot_ref[:, i * BLK:(i + 1) * BLK]

    def send_cols(j):
        dest = lax.rem(me + j, n)
        for q in range(CAP):
            colsend[dest * CAP + q] = cotb[wanted_ref[dest * CAP + q]]
        cols(j).start()

    def pair_copy(zd, c):
        return remote(ysend.at[zd, c], yrecv.at[zd, c], ys_sem.at[zd, c], yr_sem.at[zd, c], mp=pair)

    def product(slot, c):
        return lax.dot_general(
            cot_ref[...], wbuf[slot, pl.ds(pl.multiple_of(c * PIECE, PIECE), PIECE), :],
            contract_last, preferred_element_type=jnp.float32,
        ).astype(jnp.bfloat16)

    def refill(i):
        @pl.when(i + 2 < 2 * outer)
        def _():
            fetch(i + 2).start()

    def far_item(i):
        zd, _ = item_owner(i)
        slot = lax.rem(i, 2)
        fetch(i).wait()

        def one(c):
            ysend[zd, c] = product(slot, c)
            pair_copy(zd, c).start()

        loop(pieces, one)
        refill(i)

    def near_item(i):
        zd, _ = item_owner(i)
        slot = lax.rem(i, 2)
        fetch(i).wait()

        def one(c):
            own[zd, c] = product(slot, c)

        loop(pieces, one)
        refill(i)

    far_item(jnp.int32(0))
    loop(n, send_cols, 1)
    for q in range(CAP):
        colgot[me * CAP + q] = cotb[wanted_ref[me * CAP + q]]
    loop(outer, far_item, 1)

    loop(n, lambda j: lb1_in(j).wait_recv(), 1)
    lbgot[me] = lbpart[me]
    total = lbgot[0].astype(jnp.float32)
    for i in range(1, n):
        total = total + lbgot[i].astype(jnp.float32)
    lbfull[me] = total.astype(jnp.bfloat16)
    loop(n, lambda j: lb2(j).start(), 1)

    loop(2 * outer, near_item, outer)

    def up_copy(zd, c):
        return remote(own.at[zd, c], zrecv.at[zd, c], zs_sem.at[zd, c], zr_sem.at[zd, c], mp=me + INNER)

    def down_copy(zd, c):
        slot = jnp.where(zd == z - 1, outer, zd)
        return remote(own.at[zd, c], zrecv.at[slot, c], zs_sem.at[zd, c], zr_sem.at[slot, c], mp=me - INNER)

    def chain_in(slot, c):
        return remote(own.at[0, c], zrecv.at[slot, c], zs_sem.at[0, c], zr_sem.at[slot, c], mp=pair)

    def forward(s):
        zd = pick(s)
        incoming = ((zd > z) & (z > 0)) | ((zd < z) & (z < outer - 1))

        def one(c):
            pair_copy(zd, c).wait_recv()
            acc = own[zd, c].astype(jnp.float32) + yrecv[zd, c].astype(jnp.float32)

            @pl.when(incoming)
            def _():
                chain_in(zd, c).wait_recv()
                own[zd, c] = (acc + zrecv[zd, c].astype(jnp.float32)).astype(jnp.bfloat16)

            @pl.when(jnp.logical_not(incoming))
            def _():
                own[zd, c] = acc.astype(jnp.bfloat16)

            @pl.when(zd > z)
            def _():
                up_copy(zd, c).start()

            @pl.when(zd < z)
            def _():
                down_copy(zd, c).start()

        loop(pieces, one)

    loop(outer - 1, forward)

    loop(n, lambda j: lb2_in(j).wait_recv(), 1)
    both = lbfull[...].reshape(tok, 128)
    low16 = both[:, 0:64]
    back16 = (adapter_scale * both[:, 64:128].astype(jnp.float32)).astype(jnp.bfloat16)

    def dcopy():
        return remote(dsend, drecv, dps.at[0], dpr.at[0], dp=1 - core)

    def ucopy():
        return remote(usend, urecv, dps.at[1], dpr.at[1], dp=1 - core)

    def bcopy(a):
        return remote(bgsend.at[a], bgrecv.at[a], dps.at[2 + a], dpr.at[2 + a], dp=1 - core)

    dsend[...] = (
        loss_scale
        * lax.dot_general(act_ref[...], back16, contract_first, preferred_element_type=jnp.float32)
    ).astype(jnp.bfloat16)
    dcopy().start()
    usend[...] = (
        loss_scale
        * adapter_scale
        * lax.dot_general(low16, cot_ref[...], contract_first, preferred_element_type=jnp.float32)
    ).astype(jnp.bfloat16)
    ucopy().start()

    loop(n, lambda j: cols_in(j).wait_recv(), 1)
    half = MAXR * BLK // 2

    def block_row(a):
        for k in range(MAXR):
            lanes = slice(k * BLK, (k + 1) * BLK)
            cat[:, lanes] = colgot[index_ref[a * MAXR + k]] * valid_ref[a, :, lanes]
            vcat[:, k * BLK:(k + 1) * BLK] = values_ref[a, k]
        first = pl.multiple_of(a * BLK, BLK)
        act_row = act_ref[:, pl.ds(first, BLK)]
        bgtmp[...] = loss_scale * lax.dot_general(
            act_row, cat[...], contract_first, preferred_element_type=jnp.float32
        )
        bgkeep[a] = bgtmp[:, pl.ds(pl.multiple_of(core * half, half), half)]
        bgsend[a] = bgtmp[:, pl.ds(pl.multiple_of((1 - core) * half, half), half)].astype(jnp.bfloat16)
        bcopy(a).start()
        sparse[:, pl.ds(first, BLK)] = lax.dot_general(
            cat[...], vcat[...], contract_last, preferred_element_type=jnp.float32
        ) + lax.dot_general(
            back16, down_ref[pl.ds(first, BLK), :], contract_last, preferred_element_type=jnp.float32
        )

    loop(rows, block_row)

    dcopy().wait_recv()
    ucopy().wait_recv()
    down_out[...] = dsend[...].astype(jnp.float32) + drecv[...].astype(jnp.float32)
    up_out[...] = usend[...].astype(jnp.float32) + urecv[...].astype(jnp.float32)

    def block_sum(a):
        bcopy(a).wait_recv()
        for k in range(MAXR // 2):
            lanes = slice(k * BLK, (k + 1) * BLK)
            blocks_out[a, k] = bgkeep[a, :, lanes] + bgrecv[a, :, lanes].astype(jnp.float32)

    loop(rows, block_sum)

    def last(c):
        lanes = pl.ds(pl.multiple_of(c * PIECE, PIECE), PIECE)
        pair_copy(z, c).wait_recv()
        sparse[:, lanes] += own[z, c].astype(jnp.float32) + yrecv[z, c].astype(jnp.float32)

        @pl.when(z > 0)
        def _():
            chain_in(z, c).wait_recv()
            sparse[:, lanes] += zrecv[z, c].astype(jnp.float32)

        @pl.when(z < outer - 1)
        def _():
            chain_in(outer, c).wait_recv()
            sparse[:, lanes] += zrecv[outer, c].astype(jnp.float32)

        out_ref[:, lanes] = sparse[:, lanes].astype(jnp.bfloat16)

    loop(pieces, last)

    def drain(s):
        def one(c):
            pair_copy(s, c).wait_send()

            @pl.when(s > z)
            def _():
                up_copy(s, c).wait_send()

            @pl.when(s < z)
            def _():
                down_copy(s, c).wait_send()

        loop(pieces, one)

    loop(outer, drain)

    def drain_small(j):
        lb1(j).wait_send()
        lb2(j).wait_send()
        cols(j).wait_send()

    loop(n, drain_small, 1)
    dcopy().wait_send()
    ucopy().wait_send()
    loop(rows, lambda a: bcopy(a).wait_send())


def local(
    activations,
    cotangent,
    frozen_weight,
    adapter_down,
    adapter_up,
    sparse_values,
    block_cols,
    block_count,
):
    tok, wide = activations.shape
    hidden = cotangent.shape[1]
    n = lax.axis_size("mp")
    me = lax.axis_index("mp")
    per_owner = wide // BLK
    per_holder = hidden // BLK
    col_table, valid_slots, holder, slot_rank = slot_tables(
        block_cols, block_count, n, per_owner, per_holder
    )
    my_valid = lax.dynamic_index_in_dim(valid_slots, me, 0, keepdims=False)
    my_holder = lax.dynamic_index_in_dim(holder, me, 0, keepdims=False)
    my_rank = lax.dynamic_index_in_dim(slot_rank, me, 0, keepdims=False)
    recv_index = jnp.where(my_valid, my_holder * CAP + jnp.minimum(my_rank, CAP - 1), 0)
    wanted = outgoing(col_table, valid_slots, holder, slot_rank, me, per_holder)

    outer = n // INNER
    pieces = wide // PIECE
    part = tok // n
    bf, f32 = jnp.bfloat16, jnp.float32
    half = MAXR * BLK // 2
    vmem = pl.BlockSpec(memory_space=pltpu.VMEM)
    smem = pl.BlockSpec(memory_space=pltpu.SMEM)
    dma = pltpu.SemaphoreType.DMA
    return pl.pallas_call(
        functools.partial(kernel, n),
        out_shape=(
            jax.ShapeDtypeStruct((tok, wide), bf),
            jax.ShapeDtypeStruct((wide, 64), f32),
            jax.ShapeDtypeStruct((64, hidden), f32),
            jax.ShapeDtypeStruct((per_owner, MAXR // 2, BLK, BLK), f32),
        ),
        in_specs=[smem, smem, vmem, vmem, vmem, pl.BlockSpec(memory_space=pl.ANY), vmem, vmem, vmem],
        out_specs=(vmem, vmem, vmem, vmem),
        scratch_shapes=[
            pltpu.VMEM((2, wide, hidden), bf),
            pltpu.VMEM((outer, pieces, tok, PIECE), bf),
            pltpu.VMEM((outer, pieces, tok, PIECE), bf),
            pltpu.VMEM((outer, pieces, tok, PIECE), bf),
            pltpu.VMEM((outer + 1, pieces, tok, PIECE), bf),
            pltpu.VMEM((per_holder, tok, BLK), bf),
            pltpu.VMEM((n * CAP, tok, BLK), bf),
            pltpu.VMEM((n * CAP, tok, BLK), bf),
            pltpu.VMEM((tok, MAXR * BLK), bf),
            pltpu.VMEM((BLK, MAXR * BLK), bf),
            pltpu.VMEM((tok, wide), f32),
            pltpu.VMEM((BLK, MAXR * BLK), f32),
            pltpu.VMEM((per_owner, BLK, half), f32),
            pltpu.VMEM((per_owner, BLK, half), bf),
            pltpu.VMEM((per_owner, BLK, half), bf),
            pltpu.VMEM((n, part, 128), bf),
            pltpu.VMEM((n, part, 128), bf),
            pltpu.VMEM((n, part, 128), bf),
            pltpu.VMEM((wide, 64), bf),
            pltpu.VMEM((wide, 64), bf),
            pltpu.VMEM((64, hidden), bf),
            pltpu.VMEM((64, hidden), bf),
            dma((2,)),
            dma((outer, pieces)),
            dma((outer, pieces)),
            dma((outer, pieces)),
            dma((outer + 1, pieces)),
            dma((n,)),
            dma((n,)),
            dma((n,)),
            dma((n,)),
            dma((n,)),
            dma((n,)),
            dma((2 + per_owner,)),
            dma((2 + per_owner,)),
        ],
        compiler_params=pltpu.CompilerParams(
            collective_id=0, has_side_effects=True, vmem_limit_bytes=60 * 1024 * 1024
        ),
    )(
        wanted.astype(jnp.int32),
        recv_index.astype(jnp.int32),
        jnp.repeat(my_valid.reshape(per_owner, 1, MAXR).astype(bf), BLK, axis=2),
        activations,
        cotangent,
        frozen_weight,
        adapter_down,
        adapter_up,
        sparse_values,
    )


def solution(mesh):
    return jax.shard_map(
        local,
        mesh=mesh,
        in_specs=(
            P(("groups", "dp"), "mp"),
            P(("groups", "dp"), "mp"),
            P(None, "mp"),
            P("mp", None),
            P(None, "mp"),
            P("mp", None, None, None),
            P(),
            P(),
        ),
        out_specs=(
            P(("groups", "dp"), "mp"),
            P(("groups", "mp"), None),
            P("groups", "mp"),
            P(("groups", "mp"), "dp", None, None),
        ),
        check_vma=False,
    )
```

time: 338 us -> 154 us (0.46)
  waiting for transfers between devices: 226 us -> 0 us
  Pallas kernels: 0 us -> 139 us
  matrix products: 45.5 us -> 0 us
  local copies, waits for them, and re-layouts: 33.8 us -> 11.2 us
  between operations: 13.9 us -> 0.69 us
  other arithmetic: 10.7 us -> 2.45 us
  starting transfers between devices: 6.82 us -> 0 us
    reduce_scatter x1 -> x0, waiting for transfers between devices: 140 us -> none  [local(): lax.psum_scatter(lax.dot_general(frozen_weight, cotangent, contract_last,...]
    pallas_call x0 -> x1, Pallas kernels: none -> 139 us  [local(): pl.pallas_call(functools.partial(kernel, n), out_shape=(jax.ShapeDtypeStr...]
    psum x2 -> x0, waiting for transfers between devices: 85.7 us -> none  [the longest x1 85.7 us: local(): lax.psum(up_part.astype(jnp.bfloat16), 'mp').astype(jnp.float32)]
    dot_general x8 -> x0, matrix products: 45.5 us -> none  [the longest x1 21.2 us: local(): lax.dot_general(frozen_weight, cotangent, contract_last, preferred_elemen...]
    gather x3 -> x0, local copies, waits for them, and re-layouts: 18.8 us -> none  [the longest x2 16.6 us: local(): jnp.take(got_cols.reshape(-1, tok_rows, BLK), recv_index, axis=0)]
    all_to_all x1 -> x0, starting transfers between devices: 6.51 us -> none  [local(): lax.all_to_all(sent_cols, 'mp', split_axis=0, concat_axis=0, tiled=True)]
    convert_element_type x3 -> x1, other arithmetic: 4.81 us -> 0.02 us  [local(): my_valid.reshape(per_owner, 1, MAXR).astype(bf)]
    unnamed x17 -> x8, local copies, waits for them, and re-layouts: 9.68 us -> 6.1 us
  transfers between devices with their start and end apart: 4 -> 0, of which waited for: 2 -> 0; matrix products, arithmetic and copies ran while one was open for 13% -> 0% of each run, Pallas kernels for 0% -> 0%
where the time goes in v1:
time: 154 us
  Pallas kernels  139 us (90%)
  local copies, waits for them, and re-layouts  11.2 us (7%)
  other arithmetic  2.45 us (2%)
    pallas_call x1, Pallas kernels, local(): pl.pallas_call(functools.partial(kernel, n), out_shape=(jax.ShapeDtypeStr...  139 us
    unnamed x8, local copies, waits for them, and re-layouts  6.1 us

profile of v1, /device:TPU:1, one launch (start us, length us, event | category | flops | bytes accessed | tf_op | source)
XLA Modules:
  0.0 153.8 jit_solution(11377167235380553557)
XLA Ops:
  0.6 0.7 fusion.1
  1.3 0.7 reshape.151
  2.1 0.1 lt.42
  2.2 0.1 copy.20
  2.3 0.1 and.52
  2.4 0.7 broadcast_divide_fusion
  3.1 0.1 copy.21
  3.2 0.1 div.21
  3.3 0.1 reshape.152
  3.4 0.3 convert_reduce_fusion
  3.7 0.5 fusion.6.index_ref
  4.3 0.1 reshape.154
  4.5 0.6 broadcast_in_dim.41.valid_ref
  5.1 0.1 copy.22
  5.2 0.1 sub.22
  5.3 0.1 select_reduce_fusion
  5.4 0.1 copy.23
  5.5 0.6 reshape.153.wanted_ref
  6.1 1.7 %copy.25.down_ref = bf16[1024,64]{1,0:T(8,128)(2,1)} copy(bf16[1024,64]{0,1:T(8,128)(2,1)} %param.11) | data formatting | bytes 262144 | tf_op args[3]
  7.8 139.5 %shard_map.111 = (bf16[512,1024]{1,0:T(8,128)(2,1)}, f32[1024,64]{1,0:T(8,128)}, f32[64,1792]{1,0:T(8,128)}, f32[8,4,128,128]{3,2,1,0:T(8,128)}) custom-call(s32[16]{0:T(128)} %reshape.153.wanted_ref, s32[64]{0:T(128)} %fusion.6.index_ref, bf16[8,1,1024]{2,1,0:T(2,128)(2,1)} %broadcast_in_dim.41.valid_ref, bf16[512,1024]{1,0:T(8,128)(2,1)} %act_ref.1, ...), custom_call_target="tpu_custom_call" | custom-call | tf_op jit(solution)/shard_map/pallas_call | solution.py:403
  147.3 2.1 %copy.26 = f32[1024,64]{0,1:T(8,128)} copy(f32[1024,64]{1,0:T(8,128)} %get-tuple-element.13) | data formatting | bytes 524288 | tf_op jit(solution)/shard_map/pallas_call | solution.py:403
  149.4 2.3 %copy.30 = bf16[512,1024]{1,0:T(8,128)(2,1)} copy(bf16[512,1024]{1,0:T(8,128)(2,1)} %get-tuple-element.25) | data formatting | bytes 2097152
  151.7 0.8 copy.31
  152.5 1.3 copy.32
  (10 shorter events, 0.2 us)
Async XLA Ops:
  147.3 4.4 %copy-start.1 = (f32[64,1792]{1,0:T(8,128)S(1)}, f32[64,1792]{1,0:T(8,128)}, u32[]{:S(2)}) copy-start(f32[64,1792]{1,0:T(8,128)} %get-tuple-element.27) | copy-start | bytes 1376260
  147.3 5.1 %copy-start = (f32[8,4,128,128]{3,2,1,0:T(8,128)S(1)}, f32[8,4,128,128]{3,2,1,0:T(8,128)}, u32[]{:S(2)}) copy-start(f32[8,4,128,128]{3,2,1,0:T(8,128)} %get-tuple-element.28) | copy-start | bytes 6291460

commit v2 on v1

--- a/solution.py
+++ b/solution.py
@@ -20,32 +20,6 @@
 contract_first = (((0,), (0,)), ((), ()))
 
 
-def slot_tables(block_cols, block_count, mp_count, per_owner, per_holder):
-    col_table = block_cols.reshape(mp_count, per_owner * MAXR)
-    slot_ids = jnp.tile(jnp.arange(MAXR, dtype=jnp.int32), per_owner)
-    counts_wide = jnp.repeat(block_count.reshape(mp_count, per_owner), MAXR, axis=1)
-    valid_slots = slot_ids[None, :] < counts_wide
-    holder = col_table // per_holder
-    block_ids = jnp.arange(per_owner * MAXR, dtype=jnp.int32)
-    earlier = block_ids[None, :] < block_ids[:, None]
-    same_holder = (
-        (holder[:, :, None] == holder[:, None, :]) & valid_slots[:, None, :] & earlier[None, :, :]
-    )
-    slot_rank = jnp.sum(same_holder.astype(jnp.int32), axis=2)
-    return (col_table, valid_slots, holder, slot_rank)
-
-
-def outgoing(col_table, valid_slots, holder, slot_rank, my_index, per_holder):
-    capacity_ids = jnp.arange(CAP, dtype=jnp.int32)
-    picked = (
-        valid_slots[:, :, None]
-        & (holder == my_index)[:, :, None]
-        & (slot_rank[:, :, None] == capacity_ids[None, None, :])
-    )
-    local_cols = (col_table - my_index * per_holder)[:, :, None]
-    return jnp.sum(jnp.where(picked, local_cols, 0), axis=1).reshape(-1)
-
-
 def orders(outer):
     rows = []
     for z in range(outer):
@@ -55,12 +29,12 @@
 
 def kernel(
     n,
-    wanted_ref, index_ref, valid_ref,
-    act_ref, cot_ref, w_ref, down_ref, up_ref, values_ref,
+    cols_ref, count_ref,
+    act_ref, cot_ref, w_ref, down_ref, up_ref, values_hbm,
     out_ref, down_out, up_out, blocks_out,
-    wbuf, ysend, yrecv, own, zrecv, cotb, colsend, colgot, cat, vcat, sparse, bgtmp, bgkeep, bgsend, bgrecv,
+    values_ref, index_ref, wbuf, ysend, yrecv, own, zrecv, cotb, colsend, colgot, cat, vcat, sparse, bgtmp, bgkeep, bgsend, bgrecv,
     lbpart, lbgot, lbfull, dsend, drecv, usend, urecv,
-    wsem, ys_sem, yr_sem, zs_sem, zr_sem, cs_sem, cr_sem, l1s, l1r, l2s, l2r, dps, dpr,
+    vsem, wsem, ys_sem, yr_sem, zs_sem, zr_sem, cs_sem, cr_sem, l1s, l1r, l2s, l2r, dps, dpr,
 ):
     me = lax.axis_index("mp")
     core = lax.axis_index("dp")
@@ -110,7 +84,11 @@
     fetch(jnp.int32(0)).start()
     fetch(jnp.int32(1)).start()
 
-    low_part = jnp.dot(act_ref[...], down_ref[...], preferred_element_type=jnp.float32)
+    values_in = pltpu.make_async_copy(values_hbm, values_ref, vsem.at[0])
+    values_in.start()
+    low_part = lax.dot_general(
+        act_ref[...], down_ref[...], contract_last, preferred_element_type=jnp.float32
+    )
     back_part = lax.dot_general(
         cot_ref[...], up_ref[...], contract_last, preferred_element_type=jnp.float32
     )
@@ -160,10 +138,30 @@
     for i in range(cotb.shape[0]):
         cotb[i] = cot_ref[:, i * BLK:(i + 1) * BLK]
 
+    holders = cotb.shape[0]
+    shape = cols_ref.shape
+    slot_ids = lax.broadcasted_iota(jnp.int32, shape, 0)
+    row_ids = lax.broadcasted_iota(jnp.int32, shape, 1)
+    block_ids = slot_ids * shape[1] + row_ids
+    block_at = cols_ref[...]
+    used = slot_ids < count_ref[...]
+    far_code = jnp.int32(1 << 30)
+
+    def held(first_row, holder):
+        inside = (row_ids >= first_row) & (row_ids < first_row + rows)
+        return used & inside & (block_at >= holder * holders) & (block_at < (holder + 1) * holders)
+
+    def wanted(dest):
+        mine = held(dest * rows, me)
+        code = block_ids * BLK + (block_at - me * holders)
+        low_code = jnp.min(jnp.where(mine, code, far_code))
+        high_code = jnp.max(jnp.where(mine, code, 0))
+        return (low_code & (BLK - 1), high_code & (BLK - 1))
+
     def send_cols(j):
         dest = lax.rem(me + j, n)
-        for q in range(CAP):
-            colsend[dest * CAP + q] = cotb[wanted_ref[dest * CAP + q]]
+        for q, at in enumerate(wanted(dest)):
+            colsend[dest * CAP + q] = cotb[at]
         cols(j).start()
 
     def pair_copy(zd, c):
@@ -205,8 +203,9 @@
 
     far_item(jnp.int32(0))
     loop(n, send_cols, 1)
-    for q in range(CAP):
-        colgot[me * CAP + q] = cotb[wanted_ref[me * CAP + q]]
+    for q, at in enumerate(wanted(me)):
+        colgot[me * CAP + q] = cotb[at]
+    colgot[n * CAP] = jnp.zeros((tok, BLK), jnp.bfloat16)
     loop(outer, far_item, 1)
 
     loop(n, lambda j: lb1_in(j).wait_recv(), 1)
@@ -258,6 +257,16 @@
 
     loop(outer - 1, forward)
 
+    index_ref[...] = jnp.full(shape, n * CAP, jnp.int32)
+
+    def place(holder):
+        mine = held(me * rows, holder)
+        first = jnp.min(jnp.where(mine, block_ids, far_code))
+        rank = jnp.where(block_ids > first, 1, 0)
+        index_ref[...] = jnp.where(mine, holder * CAP + rank, index_ref[...])
+
+    loop(n, place)
+
     loop(n, lambda j: lb2_in(j).wait_recv(), 1)
     both = lbfull[...].reshape(tok, 128)
     low16 = both[:, 0:64]
@@ -274,7 +283,7 @@
 
     dsend[...] = (
         loss_scale
-        * lax.dot_general(act_ref[...], back16, contract_first, preferred_element_type=jnp.float32)
+        * lax.dot_general(back16, act_ref[...], contract_first, preferred_element_type=jnp.float32)
     ).astype(jnp.bfloat16)
     dcopy().start()
     usend[...] = (
@@ -284,13 +293,15 @@
     ).astype(jnp.bfloat16)
     ucopy().start()
 
+    values_in.wait()
     loop(n, lambda j: cols_in(j).wait_recv(), 1)
     half = MAXR * BLK // 2
 
     def block_row(a):
         for k in range(MAXR):
             lanes = slice(k * BLK, (k + 1) * BLK)
-            cat[:, lanes] = colgot[index_ref[a * MAXR + k]] * valid_ref[a, :, lanes]
+            here = (slot_ids == k) & (row_ids == me * rows + a)
+            cat[:, lanes] = colgot[jnp.sum(jnp.where(here, index_ref[...], 0))]
             vcat[:, k * BLK:(k + 1) * BLK] = values_ref[a, k]
         first = pl.multiple_of(a * BLK, BLK)
         act_row = act_ref[:, pl.ds(first, BLK)]
@@ -302,9 +313,7 @@
         bcopy(a).start()
         sparse[:, pl.ds(first, BLK)] = lax.dot_general(
             cat[...], vcat[...], contract_last, preferred_element_type=jnp.float32
-        ) + lax.dot_general(
-            back16, down_ref[pl.ds(first, BLK), :], contract_last, preferred_element_type=jnp.float32
-        )
+        ) + jnp.dot(back16, down_ref[:, pl.ds(first, BLK)], preferred_element_type=jnp.float32)
 
     loop(rows, block_row)
 
@@ -380,37 +389,29 @@
     tok, wide = activations.shape
     hidden = cotangent.shape[1]
     n = lax.axis_size("mp")
-    me = lax.axis_index("mp")
     per_owner = wide // BLK
     per_holder = hidden // BLK
-    col_table, valid_slots, holder, slot_rank = slot_tables(
-        block_cols, block_count, n, per_owner, per_holder
-    )
-    my_valid = lax.dynamic_index_in_dim(valid_slots, me, 0, keepdims=False)
-    my_holder = lax.dynamic_index_in_dim(holder, me, 0, keepdims=False)
-    my_rank = lax.dynamic_index_in_dim(slot_rank, me, 0, keepdims=False)
-    recv_index = jnp.where(my_valid, my_holder * CAP + jnp.minimum(my_rank, CAP - 1), 0)
-    wanted = outgoing(col_table, valid_slots, holder, slot_rank, me, per_holder)
-
     outer = n // INNER
     pieces = wide // PIECE
     part = tok // n
     bf, f32 = jnp.bfloat16, jnp.float32
     half = MAXR * BLK // 2
     vmem = pl.BlockSpec(memory_space=pltpu.VMEM)
-    smem = pl.BlockSpec(memory_space=pltpu.SMEM)
+    anywhere = pl.BlockSpec(memory_space=pl.ANY)
     dma = pltpu.SemaphoreType.DMA
-    return pl.pallas_call(
+    input_grad, down_turned, up_grad, block_grads = pl.pallas_call(
         functools.partial(kernel, n),
         out_shape=(
             jax.ShapeDtypeStruct((tok, wide), bf),
-            jax.ShapeDtypeStruct((wide, 64), f32),
+            jax.ShapeDtypeStruct((64, wide), f32),
             jax.ShapeDtypeStruct((64, hidden), f32),
             jax.ShapeDtypeStruct((per_owner, MAXR // 2, BLK, BLK), f32),
         ),
-        in_specs=[smem, smem, vmem, vmem, vmem, pl.BlockSpec(memory_space=pl.ANY), vmem, vmem, vmem],
+        in_specs=[vmem, vmem, vmem, vmem, anywhere, vmem, vmem, anywhere],
         out_specs=(vmem, vmem, vmem, vmem),
         scratch_shapes=[
+            pltpu.VMEM(sparse_values.shape, bf),
+            pltpu.VMEM(block_cols.shape[::-1], jnp.int32),
             pltpu.VMEM((2, wide, hidden), bf),
             pltpu.VMEM((outer, pieces, tok, PIECE), bf),
             pltpu.VMEM((outer, pieces, tok, PIECE), bf),
@@ -418,7 +419,7 @@
             pltpu.VMEM((outer + 1, pieces, tok, PIECE), bf),
             pltpu.VMEM((per_holder, tok, BLK), bf),
             pltpu.VMEM((n * CAP, tok, BLK), bf),
-            pltpu.VMEM((n * CAP, tok, BLK), bf),
+            pltpu.VMEM((n * CAP + 1, tok, BLK), bf),
             pltpu.VMEM((tok, MAXR * BLK), bf),
             pltpu.VMEM((BLK, MAXR * BLK), bf),
             pltpu.VMEM((tok, wide), f32),
@@ -429,10 +430,11 @@
             pltpu.VMEM((n, part, 128), bf),
             pltpu.VMEM((n, part, 128), bf),
             pltpu.VMEM((n, part, 128), bf),
-            pltpu.VMEM((wide, 64), bf),
-            pltpu.VMEM((wide, 64), bf),
+            pltpu.VMEM((64, wide), bf),
+            pltpu.VMEM((64, wide), bf),
             pltpu.VMEM((64, hidden), bf),
             pltpu.VMEM((64, hidden), bf),
+            dma((1,)),
             dma((2,)),
             dma((outer, pieces)),
             dma((outer, pieces)),
@@ -451,16 +453,16 @@
             collective_id=0, has_side_effects=True, vmem_limit_bytes=60 * 1024 * 1024
         ),
     )(
-        wanted.astype(jnp.int32),
-        recv_index.astype(jnp.int32),
-        jnp.repeat(my_valid.reshape(per_owner, 1, MAXR).astype(bf), BLK, axis=2),
+        block_cols.T,
+        block_count.reshape(1, -1),
         activations,
         cotangent,
         frozen_weight,
-        adapter_down,
+        adapter_down.T,
         adapter_up,
         sparse_values,
     )
+    return input_grad, down_turned.T, up_grad, block_grads
 
 
 def solution(mesh):

time: 154 us -> 146 us (0.948)
  local copies, waits for them, and re-layouts: 11.2 us -> 6.18 us
  other arithmetic: 2.45 us -> 0 us
    pallas_call x1 -> x0, local copies, waits for them, and re-layouts: 2.08 us -> none  [local(): pl.pallas_call(functools.partial(kernel, n), out_shape=(jax.ShapeDtypeStr...]
where the time goes in v2:
time: 146 us
  Pallas kernels  139 us (95%)
  local copies, waits for them, and re-layouts  6.18 us (4%)
    pallas_call x1, Pallas kernels, local(): pl.pallas_call(functools.partial(kernel, n), out_shape=(jax.ShapeDtypeStr...  139 us
    unnamed x8, local copies, waits for them, and re-layouts  6.18 us

profile of v2, /device:TPU:1, one launch (start us, length us, event | category | flops | bytes accessed | tf_op | source)
XLA Modules:
  0.0 145.8 jit_solution(11582517435850162994)
XLA Ops:
  0.6 138.9 %shard_map.111 = (bf16[512,1024]{1,0:T(8,128)(2,1)}, f32[64,1024]{1,0:T(8,128)}, f32[64,1792]{1,0:T(8,128)}, f32[8,4,128,128]{3,2,1,0:T(8,128)}) custom-call(s32[8,64]{1,0:T(8,128)} %bitcast.6, s32[1,64]{1,0:T(1,128)} %bitcast.7, bf16[512,1024]{1,0:T(8,128)(2,1)} %act_ref.1, bf16[512,1792]{1,0:T(8,128)(2,1)} %cot_ref.1, bf16[8192,1792]{1,0:T(8,128)(2,1)} %w_ref.1, ...), custom_call_target="tpu_custom_call" | custom-call | tf_op jit(solution)/shard_map/pallas_call | solution.py:402
  139.6 0.0 copy-start.1
  139.6 0.0 copy-start
  139.6 2.4 %copy.16 = bf16[512,1024]{1,0:T(8,128)(2,1)} copy(bf16[512,1024]{1,0:T(8,128)(2,1)} %get-tuple-element.16) | data formatting | bytes 2097152
  142.0 1.7 %copy.17 = f32[1024,64]{0,1:T(8,128)} copy(f32[1024,64]{0,1:T(8,128)} %bitcast.4) | data formatting | bytes 524288
  143.7 0.0 copy-done.1
  143.7 0.8 copy.18
  144.5 0.0 copy-done
  144.5 1.3 copy.19
Async XLA Ops:
  139.6 4.1 %copy-start.1 = (f32[64,1792]{1,0:T(8,128)S(1)}, f32[64,1792]{1,0:T(8,128)}, u32[]{:S(2)}) copy-start(f32[64,1792]{1,0:T(8,128)} %get-tuple-element.18) | copy-start | bytes 1376260
  139.6 4.9 %copy-start = (f32[8,4,128,128]{3,2,1,0:T(8,128)S(1)}, f32[8,4,128,128]{3,2,1,0:T(8,128)}, u32[]{:S(2)}) copy-start(f32[8,4,128,128]{3,2,1,0:T(8,128)} %get-tuple-element.19) | copy-start | bytes 6291460

commit v3 on v2

--- a/solution.py
+++ b/solution.py
@@ -32,9 +32,9 @@
     cols_ref, count_ref,
     act_ref, cot_ref, w_ref, down_ref, up_ref, values_hbm,
     out_ref, down_out, up_out, blocks_out,
-    values_ref, index_ref, wbuf, ysend, yrecv, own, zrecv, cotb, colsend, colgot, cat, vcat, sparse, bgtmp, bgkeep, bgsend, bgrecv,
+    values_ref, index_ref, wbuf, ysend, yrecv, own, zrecv, crossrecv, cotb, colsend, colgot, cat, vcat, sparse, bgtmp, bgkeep, bgsend, bgrecv,
     lbpart, lbgot, lbfull, dsend, drecv, usend, urecv,
-    vsem, wsem, ys_sem, yr_sem, zs_sem, zr_sem, cs_sem, cr_sem, l1s, l1r, l2s, l2r, dps, dpr,
+    vsem, wsem, ys_sem, yr_sem, zs_sem, zr_sem, xs_sem, xr_sem, cs_sem, cr_sem, l1s, l1r, l2s, l2r, dps, dpr,
 ):
     me = lax.axis_index("mp")
     core = lax.axis_index("dp")
@@ -178,6 +178,12 @@
         def _():
             fetch(i + 2).start()
 
+    def edge(zd, c):
+        return ((zd == 0) | (zd == outer - 1)) & (c == pieces - 1)
+
+    def chain_first(zd, c):
+        return edge(zd, c) & (zd != z)
+
     def far_item(i):
         zd, _ = item_owner(i)
         slot = lax.rem(i, 2)
@@ -185,7 +191,10 @@
 
         def one(c):
             ysend[zd, c] = product(slot, c)
-            pair_copy(zd, c).start()
+
+            @pl.when(jnp.logical_not(edge(zd, c)))
+            def _():
+                pair_copy(zd, c).start()
 
         loop(pieces, one)
         refill(i)
@@ -228,22 +237,62 @@
     def chain_in(slot, c):
         return remote(own.at[0, c], zrecv.at[slot, c], zs_sem.at[0, c], zr_sem.at[slot, c], mp=pair)
 
+    def cross(slot):
+        zd = slot * (outer - 1)
+        ahead = jnp.where(zd > z, me + INNER, me - INNER)
+        return remote(
+            ysend.at[zd, pieces - 1], crossrecv.at[slot], xs_sem.at[slot], xr_sem.at[slot], mp=ahead
+        )
+
+    def cross_in(slot):
+        return remote(
+            ysend.at[0, 0], crossrecv.at[slot], xs_sem.at[slot], xr_sem.at[slot], mp=pair
+        )
+
+    def cross_add(slot, zd):
+        cross_in(slot).wait_recv()
+        ysend[zd, pieces - 1] = (
+            ysend[zd, pieces - 1].astype(jnp.float32) + crossrecv[slot].astype(jnp.float32)
+        ).astype(jnp.bfloat16)
+
     def forward(s):
         zd = pick(s)
         incoming = ((zd > z) & (z > 0)) | ((zd < z) & (z < outer - 1))
 
         def one(c):
-            pair_copy(zd, c).wait_recv()
-            acc = own[zd, c].astype(jnp.float32) + yrecv[zd, c].astype(jnp.float32)
-
-            @pl.when(incoming)
-            def _():
-                chain_in(zd, c).wait_recv()
-                own[zd, c] = (acc + zrecv[zd, c].astype(jnp.float32)).astype(jnp.bfloat16)
-
-            @pl.when(jnp.logical_not(incoming))
-            def _():
-                own[zd, c] = acc.astype(jnp.bfloat16)
+            direct = chain_first(zd, c)
+            slot = jnp.where(zd == 0, 0, 1)
+
+            @pl.when(direct)
+            def _():
+                @pl.when(incoming)
+                def _():
+                    cross_add(slot, zd)
+                    chain_in(zd, c).wait_recv()
+                    own[zd, c] = (
+                        own[zd, c].astype(jnp.float32) + zrecv[zd, c].astype(jnp.float32)
+                    ).astype(jnp.bfloat16)
+
+                cross(slot).start()
+
+            @pl.when(jnp.logical_not(direct))
+            def _():
+                pair_copy(zd, c).wait_recv()
+
+                @pl.when(incoming)
+                def _():
+                    chain_in(zd, c).wait_recv()
+                    own[zd, c] = (
+                        own[zd, c].astype(jnp.float32)
+                        + yrecv[zd, c].astype(jnp.float32)
+                        + zrecv[zd, c].astype(jnp.float32)
+                    ).astype(jnp.bfloat16)
+
+                @pl.when(jnp.logical_not(incoming))
+                def _():
+                    own[zd, c] = (
+                        own[zd, c].astype(jnp.float32) + yrecv[zd, c].astype(jnp.float32)
+                    ).astype(jnp.bfloat16)
 
             @pl.when(zd > z)
             def _():
@@ -256,6 +305,11 @@
         loop(pieces, one)
 
     loop(outer - 1, forward)
+
+    @pl.when(edge(z, pieces - 1))
+    def _():
+        cross_add(jnp.where(z == 0, 0, 1), z)
+        pair_copy(z, pieces - 1).start()
 
     index_ref[...] = jnp.full(shape, n * CAP, jnp.int32)
 
@@ -351,7 +405,13 @@
 
     def drain(s):
         def one(c):
-            pair_copy(s, c).wait_send()
+            @pl.when(jnp.logical_not(chain_first(s, c)))
+            def _():
+                pair_copy(s, c).wait_send()
+
+            @pl.when(chain_first(s, c))
+            def _():
+                cross(jnp.where(s == 0, 0, 1)).wait_send()
 
             @pl.when(s > z)
             def _():
@@ -417,6 +477,7 @@
             pltpu.VMEM((outer, pieces, tok, PIECE), bf),
             pltpu.VMEM((outer, pieces, tok, PIECE), bf),
             pltpu.VMEM((outer + 1, pieces, tok, PIECE), bf),
+            pltpu.VMEM((2, tok, PIECE), bf),
             pltpu.VMEM((per_holder, tok, BLK), bf),
             pltpu.VMEM((n * CAP, tok, BLK), bf),
             pltpu.VMEM((n * CAP + 1, tok, BLK), bf),
@@ -440,6 +501,8 @@
             dma((outer, pieces)),
             dma((outer, pieces)),
             dma((outer + 1, pieces)),
+            dma((2,)),
+            dma((2,)),
             dma((n,)),
             dma((n,)),
             dma((n,)),

time: 146 us -> 135 us (0.925)
  Pallas kernels: 139 us -> 128 us
    pallas_call x1, Pallas kernels: 139 us -> 128 us  [local(): pl.pallas_call(functools.partial(kernel, n), out_shape=(jax.ShapeDtypeStr...]
where the time goes in v3:
time: 135 us
  Pallas kernels  128 us (95%)
  local copies, waits for them, and re-layouts  6.18 us (5%)
    pallas_call x1, Pallas kernels, local(): pl.pallas_call(functools.partial(kernel, n), out_shape=(jax.ShapeDtypeStr...  128 us
    unnamed x8, local copies, waits for them, and re-layouts  6.18 us

profile of v3, /device:TPU:1, one launch (start us, length us, event | category | flops | bytes accessed | tf_op | source)
XLA Modules:
  0.0 135.1 jit_solution(1446776943222128285)
XLA Ops:
  0.6 128.3 %shard_map.111 = (bf16[512,1024]{1,0:T(8,128)(2,1)}, f32[64,1024]{1,0:T(8,128)}, f32[64,1792]{1,0:T(8,128)}, f32[8,4,128,128]{3,2,1,0:T(8,128)}) custom-call(s32[8,64]{1,0:T(8,128)} %bitcast.6, s32[1,64]{1,0:T(1,128)} %bitcast.7, bf16[512,1024]{1,0:T(8,128)(2,1)} %act_ref.1, bf16[512,1792]{1,0:T(8,128)(2,1)} %cot_ref.1, bf16[8192,1792]{1,0:T(8,128)(2,1)} %w_ref.1, ...), custom_call_target="tpu_custom_call" | custom-call | tf_op jit(solution)/shard_map/pallas_call | solution.py:462
  128.9 0.0 copy-start.1
  128.9 0.0 copy-start
  128.9 2.4 %copy.16 = bf16[512,1024]{1,0:T(8,128)(2,1)} copy(bf16[512,1024]{1,0:T(8,128)(2,1)} %get-tuple-element.16) | data formatting | bytes 2097152
  131.3 1.7 %copy.17 = f32[1024,64]{0,1:T(8,128)} copy(f32[1024,64]{0,1:T(8,128)} %bitcast.4) | data formatting | bytes 524288
  133.0 0.0 copy-done.1
  133.0 0.8 copy.18
  133.8 0.0 copy-done
  133.8 1.3 copy.19
Async XLA Ops:
  128.9 4.1 %copy-start.1 = (f32[64,1792]{1,0:T(8,128)S(1)}, f32[64,1792]{1,0:T(8,128)}, u32[]{:S(2)}) copy-start(f32[64,1792]{1,0:T(8,128)} %get-tuple-element.18) | copy-start | bytes 1376260
  128.9 4.9 %copy-start = (f32[8,4,128,128]{3,2,1,0:T(8,128)S(1)}, f32[8,4,128,128]{3,2,1,0:T(8,128)}, u32[]{:S(2)}) copy-start(f32[8,4,128,128]{3,2,1,0:T(8,128)} %get-tuple-element.19) | copy-start | bytes 6291460
